TPU v7x, 256 devices: a whole 4x4x8 slice. The times are simulated.
256 devices in a mesh: mirror: 4 (over x), expert: 64 (over y, z, core).
Axes of the slice: x: 4, y: 4, z: 8, core: 2. Of those that a mesh axis runs over, the one named last changes fastest.
Arguments:
- tokens: bfloat16 [32768, 1536], P(('mirror', 'expert')), may hold values from -6 to 6
- routes: int32 [32768, 8], P(('mirror', 'expert')), may hold values from 0 to 63, all different within a row; in each aligned block of 128 rows (0 to 127, 128 to 255, ...) at most 20 rows name the same one
- gate_probs: float32 [32768, 8], P(('mirror', 'expert')), may hold values from 0.05 to 0.3
- cotangent: bfloat16 [32768, 1536], P(('mirror', 'expert')), may hold values from -1.5 to 1.5
- w_gate: bfloat16 [64, 1536, 384], P('expert'), may hold values from -0.15625 to 0.15625
- w_up: bfloat16 [64, 1536, 384], P('expert'), may hold values from -0.15625 to 0.15625
- w_down: bfloat16 [64, 384, 1536], P('expert'), may hold values from -0.3125 to 0.3125
Outputs:
- layer_out: bfloat16 [32768, 1536], P(('mirror', 'expert'))
- grad_tokens: bfloat16 [32768, 1536], P(('mirror', 'expert'))
- grad_probs: float32 [32768, 8], P(('mirror', 'expert'))
- grad_w_gate: float32 [64, 1536, 384], P('expert', 'mirror')
- grad_w_up: float32 [64, 1536, 384], P('expert', 'mirror')
- grad_w_down: float32 [64, 384, 1536], P('expert', None, 'mirror')
Inputs may be any that keep to these rules, and one draw needn't show every extreme that they name: `routes`: each row names 8 different experts. In the rows of one device no expert is named more than 20 times, and in every draw some device has an expert named exactly 20 times.
All inputs are finite; a program needn't handle non-finite values.
Results may differ from a plain program's by a relative error of at most 0.012.
Values may be sent and summed in bfloat16 or wider, within the bound.
A program may use at most 128 MiB of HBM per device.

v0:
```python
import jax
import jax.numpy as jnp
from jax import lax
from jax.sharding import PartitionSpec as P


def shards(tokens, routes, gate_probs, cotangent, w_gate, w_up, w_down):
    experts = lax.axis_size("expert")
    token_count = tokens.shape[0]
    top_count = routes.shape[1]
    model_width = tokens.shape[1]
    route_count = token_count * top_count
    capacity = min(token_count, token_count * top_count // experts * 5 // 4)
    flat_routes = routes.reshape(route_count)
    one_hot = (flat_routes[:, None] == jnp.arange(experts, dtype=jnp.int32)[None, :]).astype(
        jnp.int32
    )
    slot_index = jnp.sum(one_hot * jnp.cumsum(one_hot, axis=0), axis=1) - 1
    destination = flat_routes * capacity + slot_index
    slot_total = experts * capacity
    repeated = jnp.repeat(tokens, top_count, axis=0)
    outgoing = jnp.zeros((slot_total, model_width), jnp.bfloat16).at[destination].set(repeated)
    arrived = lax.all_to_all(
        outgoing.reshape(experts, capacity, model_width),
        "expert",
        split_axis=0,
        concat_axis=0,
        tiled=True,
    )
    expert_rows = arrived.reshape(slot_total, model_width)
    gate_mat = w_gate[0]
    up_mat = w_up[0]
    down_mat = w_down[0]
    pre_gate = jnp.dot(expert_rows, gate_mat, preferred_element_type=jnp.float32)
    pre_up = jnp.dot(expert_rows, up_mat, preferred_element_type=jnp.float32)
    sigmoid_gate = jax.nn.sigmoid(pre_gate)
    hidden = (pre_gate * sigmoid_gate * pre_up).astype(jnp.bfloat16)
    expert_out = jnp.dot(hidden, down_mat, preferred_element_type=jnp.float32).astype(jnp.bfloat16)
    out_blocks = expert_out.reshape(experts, capacity, model_width)
    flat_probs = gate_probs.reshape(route_count, 1)
    scaled = (flat_probs * jnp.repeat(cotangent, top_count, axis=0).astype(jnp.float32)).astype(
        jnp.bfloat16
    )
    grad_outgoing = jnp.zeros((slot_total, model_width), jnp.bfloat16).at[destination].set(scaled)
    grad_blocks = grad_outgoing.reshape(experts, capacity, model_width)
    returned = lax.all_to_all(out_blocks, "expert", split_axis=0, concat_axis=0, tiled=True)
    grad_arrived = lax.all_to_all(grad_blocks, "expert", split_axis=0, concat_axis=0, tiled=True)
    out_route = returned.reshape(slot_total, model_width)[destination].reshape(
        token_count, top_count, model_width
    )
    layer_out = jnp.einsum("tk,tkd->td", gate_probs, out_route.astype(jnp.float32)).astype(
        jnp.bfloat16
    )
    grad_probs = jnp.einsum("tkd,td->tk", out_route, cotangent, preferred_element_type=jnp.float32)
    scaled_rows = grad_arrived.reshape(slot_total, model_width)
    grad_hidden = lax.dot_general(
        scaled_rows, down_mat, (((1,), (1,)), ((), ())), preferred_element_type=jnp.float32
    )
    grad_pre_gate = (
        grad_hidden * pre_up * sigmoid_gate * (1.0 + pre_gate * (1.0 - sigmoid_gate))
    ).astype(jnp.bfloat16)
    grad_pre_up = (grad_hidden * pre_gate * sigmoid_gate).astype(jnp.bfloat16)
    grad_route = (
        lax.dot_general(
            grad_pre_gate, gate_mat, (((1,), (1,)), ((), ())), preferred_element_type=jnp.float32
        )
        + lax.dot_general(
            grad_pre_up, up_mat, (((1,), (1,)), ((), ())), preferred_element_type=jnp.float32
        )
    ).astype(jnp.bfloat16)
    grad_back = lax.all_to_all(
        grad_route.reshape(experts, capacity, model_width),
        "expert",
        split_axis=0,
        concat_axis=0,
        tiled=True,
    )
    grad_per_route = grad_back.reshape(slot_total, model_width)[destination].reshape(
        token_count, top_count, model_width
    )
    grad_tokens = jnp.sum(grad_per_route.astype(jnp.float32), axis=1).astype(jnp.bfloat16)
    hidden_width = gate_mat.shape[1]
    gate_part = lax.dot_general(
        expert_rows, grad_pre_gate, (((0,), (0,)), ((), ())), preferred_element_type=jnp.float32
    )
    up_part = lax.dot_general(
        expert_rows, grad_pre_up, (((0,), (0,)), ((), ())), preferred_element_type=jnp.float32
    )
    down_part = lax.dot_general(
        scaled_rows, hidden, (((0,), (0,)), ((), ())), preferred_element_type=jnp.float32
    )
    summed = lax.psum_scatter(
        jnp.concatenate([gate_part, up_part, down_part], axis=1).astype(jnp.bfloat16),
        "mirror",
        scatter_dimension=0,
        tiled=True,
    ).astype(jnp.float32)
    grad_w_gate = summed[:, :hidden_width][None]
    grad_w_up = summed[:, hidden_width : 2 * hidden_width][None]
    grad_w_down = summed[:, 2 * hidden_width :].T[None]
    return (layer_out, grad_tokens, grad_probs, grad_w_gate, grad_w_up, grad_w_down)


def solution(mesh):
    placed = (
        P(("mirror", "expert"), None),
        P(("mirror", "expert"), None),
        P(("mirror", "expert"), None),
        P(("mirror", "expert"), None),
        P("expert", None, None),
        P("expert", None, None),
        P("expert", None, None),
    )
    return jax.shard_map(
        shards,
        mesh=mesh,
        in_specs=placed,
        out_specs=(
            P(("mirror", "expert"), None),
            P(("mirror", "expert"), None),
            P(("mirror", "expert"), None),
            P("expert", "mirror", None),
            P("expert", "mirror", None),
            P("expert", None, "mirror"),
        ),
        check_vma=False,
    )
```

profile of v0, /device:TPU:1, one launch (start us, length us, event | category | flops | bytes accessed | tf_op | source)
XLA Modules:
  0.0 557.7 jit_solution(7674607675394110688)
XLA Ops:
  7.2 0.8 broadcast_multiply_fusion
  8.0 0.8 copy.24
  9.2 18.0 %reduce-window.6 = s32[64,8,128]{2,1,0:T(8,128)S(1)} reduce-window(s32[64,8,128]{2,1,0:T(8,128)S(1)} %fusion.28, s32[]{:T(128)} %constant.8.clone.1), window={size=1x1x128 pad=0_0x0_0x127_0}, to_apply=%region_0.0 | reduce-window | flops 8323072 | bytes 524292 | tf_op jit(solution)/shard_map/reduce-window
  27.3 0.1 copy.26
  27.6 0.1 broadcast_add_fusion
  27.8 8.2 %scatter_custom_fusion = bf16[1280,1536]{1,0:T(8,128)(2,1)} fusion(s32[1024]{0:T(1024)S(1)} %bitcast.83, bf16[]{:T(256)} %constant.6.clone.1, bf16[128,1536]{1,0:T(8,128)(2,1)} %param.7), kind=kCustom, calls=%fused_computation.16 | custom fusion | bytes 4325378 | tf_op jit(solution)/shard_map/scatter | solution.py:22
  36.0 6.8 %reshape.102 = bf16[64,20,1536]{2,1,0:T(8,128)(2,1)} reshape(bf16[1280,1536]{1,0:T(8,128)(2,1)} %scatter_custom_fusion) | data formatting | bytes 7864320 | tf_op jit(solution)/shard_map/reshape | solution.py:24
  42.8 13.5 %all-to-all-start = ((bf16[64,20,1536]{2,1,0:T(8,128)(2,1)}), bf16[64,20,1536]{2,1,0:T(8,128)(2,1)}, u32[]{:S(2)}, u32[]{:S(2)}) async-start(bf16[64,20,1536]{2,1,0:T(8,128)(2,1)} %reshape.102), calls=%async_computation | async-start | bytes 9437184 | tf_op jit(solution)/shard_map/all_to_all | solution.py:23
  56.5 8.3 %scatter_custom_fusion.1 = bf16[1280,1536]{1,0:T(8,128)(2,1)} fusion(s32[1024]{0:T(1024)S(1)} %bitcast.84, f32[128,1536]{1,0:T(8,128)S(1)} %convert_element_type.44, f32[1024]{0:T(1024)S(1)} %mul.59, bf16[]{:T(256)} %constant.6.clone.1), kind=kCustom, calls=%fused_computation.10 | custom fusion | flops 3145728 | bytes 4722690 | tf_op jit(solution)/shard_map/scatter | solution.py:44
  64.8 6.8 %reshape.107 = bf16[64,20,1536]{2,1,0:T(8,128)(2,1)} reshape(bf16[1280,1536]{1,0:T(8,128)(2,1)} %scatter_custom_fusion.1) | data formatting | bytes 7864320 | tf_op jit(solution)/shard_map/reshape | solution.py:45
  71.7 91.7 %all-to-all-done = bf16[64,20,1536]{2,1,0:T(8,128)(2,1)} async-done(((bf16[64,20,1536]{2,1,0:T(8,128)(2,1)}), bf16[64,20,1536]{2,1,0:T(8,128)(2,1)}, u32[]{:S(2)}, u32[]{:S(2)}) %all-to-all-start) | async-done | bytes 3932192 | tf_op jit(solution)/shard_map/all_to_all | solution.py:23
  163.4 6.0 %all-to-all-start.2 = ((bf16[64,20,1536]{2,1,0:T(8,128)(2,1)}), bf16[64,20,1536]{2,1,0:T(8,128)(2,1)}, u32[]{:S(2)}, u32[]{:S(2)}) async-start(bf16[64,20,1536]{2,1,0:T(8,128)(2,1)} %reshape.107), calls=%async_computation.2 | async-start | bytes 9437184 | tf_op jit(solution)/shard_map/all_to_all | solution.py:47
  169.4 6.9 %reshape.103 = bf16[1280,1536]{1,0:T(8,128)(2,1)} reshape(bf16[64,20,1536]{2,1,0:T(8,128)(2,1)} %all-to-all-done) | data formatting | bytes 7864320 | tf_op jit(solution)/shard_map/reshape | solution.py:30
  176.3 6.1 %fusion.19 = f32[1280,384]{1,0:T(8,128)} fusion(bf16[1280,1536]{1,0:T(8,128)(2,1)} %reshape.103, bf16[1,1536,384]{2,1,0:T(8,128)(2,1)} %param.12), kind=kOutput, calls=%fused_computation.34 | convolution fusion | flops 1509949440 | bytes 7077888 | tf_op jit(solution)/shard_map/dot_general | solution.py:35
  182.4 3.6 fusion.23
  186.0 90.5 %all-to-all-done.2 = bf16[64,20,1536]{2,1,0:T(8,128)(2,1)} async-done(((bf16[64,20,1536]{2,1,0:T(8,128)(2,1)}), bf16[64,20,1536]{2,1,0:T(8,128)(2,1)}, u32[]{:S(2)}, u32[]{:S(2)}) %all-to-all-start.2) | async-done | bytes 3932192 | tf_op jit(solution)/shard_map/all_to_all | solution.py:47
  276.6 6.9 %reshape.108 = bf16[1280,1536]{1,0:T(8,128)(2,1)} reshape(bf16[64,20,1536]{2,1,0:T(8,128)(2,1)} %all-to-all-done.2) | data formatting | bytes 7864320 | tf_op jit(solution)/shard_map/reshape | solution.py:55
  283.5 7.2 %multiply_convert_fusion = (bf16[1280,384]{1,0:T(8,128)(2,1)}, bf16[1280,384]{1,0:T(8,128)(2,1)S(1)}, bf16[1280,384]{1,0:T(8,128)(2,1)S(1)}) fusion(f32[1280,384]{1,0:T(8,128)} %fusion.23, f32[1280,384]{1,0:T(8,128)} %fusion.19, bf16[1280,1536]{1,0:T(8,128)(2,1)} %reshape.108, bf16[1,384,1536]{2,1,0:T(8,128)(2,1)S(1)} %copy-done), kind=kOutput, calls=%fused_computation.23 | convolution fusion | flops 1517813760 | bytes 11993088 | tf_op jit(solution)/shard_map/dot_general | solution.py:56
  290.7 0.9 copy-done.12
  291.6 4.1 convolution_convert_fusion
  295.7 6.8 %reshape.104 = bf16[64,20,1536]{2,1,0:T(8,128)(2,1)} reshape(bf16[1280,1536]{1,0:T(8,128)(2,1)} %convolution_convert_fusion) | data formatting | bytes 7864320 | tf_op jit(solution)/shard_map/reshape | solution.py:39
  302.5 6.0 %all-to-all-start.1 = ((bf16[64,20,1536]{2,1,0:T(8,128)(2,1)}), bf16[64,20,1536]{2,1,0:T(8,128)(2,1)}, u32[]{:S(2)}, u32[]{:S(2)}) async-start(bf16[64,20,1536]{2,1,0:T(8,128)(2,1)} %reshape.104), calls=%async_computation.1 | async-start | bytes 9437184 | tf_op jit(solution)/shard_map/all_to_all | solution.py:46
  308.5 0.2 reduce-scatter.4.cloned.1.call-start
  308.8 4.3 convolution_convert_fusion.1
  313.1 1.7 convolution_convert_fusion.2
  314.8 1.7 convolution_convert_fusion.3
  316.5 2.1 pad_maximum_fusion
  318.6 5.8 %copy.35 = bf16[1536,1152]{1,0:T(8,128)(2,1)} copy(bf16[1536,1152]{0,1:T(8,128)(2,1)} %pad_maximum_fusion) | data formatting | bytes 7077888
  324.5 2.3 fusion.21
  326.7 4.2 fusion
  330.9 6.8 %reshape.109 = bf16[64,20,1536]{2,1,0:T(8,128)(2,1)} reshape(bf16[1280,1536]{1,0:T(8,128)(2,1)} %fusion) | data formatting | bytes 7864320 | tf_op jit(solution)/shard_map/reshape | solution.py:72
  337.7 78.0 %all-to-all-done.1 = bf16[64,20,1536]{2,1,0:T(8,128)(2,1)} async-done(((bf16[64,20,1536]{2,1,0:T(8,128)(2,1)}), bf16[64,20,1536]{2,1,0:T(8,128)(2,1)}, u32[]{:S(2)}, u32[]{:S(2)}) %all-to-all-start.1) | async-done | bytes 3932192 | tf_op jit(solution)/shard_map/all_to_all | solution.py:46
  415.7 6.4 %all-to-all-start.3 = ((bf16[64,20,1536]{2,1,0:T(8,128)(2,1)}), bf16[64,20,1536]{2,1,0:T(8,128)(2,1)}, u32[]{:S(2)}, u32[]{:S(2)}) async-start(bf16[64,20,1536]{2,1,0:T(8,128)(2,1)} %reshape.109), calls=%async_computation.3 | async-start | bytes 9437184 | tf_op jit(solution)/shard_map/all_to_all | solution.py:71
  422.1 0.1 copy.31
  422.3 1.8 copy.36
  424.2 0.9 slice_bitcast_fusion
  425.1 1.0 copy.30
  426.1 1.0 copy.29
  427.2 6.9 %reshape.105 = bf16[1280,1536]{1,0:T(8,128)(2,1)} reshape(bf16[64,20,1536]{2,1,0:T(8,128)(2,1)} %all-to-all-done.1) | data formatting | bytes 7864320 | tf_op jit(solution)/shard_map/reshape | solution.py:48
  434.1 9.9 %gather_fusion = bf16[1024,1536]{1,0:T(8,128)(2,1)} fusion(bf16[1280,1536]{1,0:T(8,128)(2,1)} %reshape.105, s32[1024]{0:T(1024)S(1)} %broadcast_clamp_fusion), kind=kCustom, calls=%fused_computation | custom fusion | bytes 6295552 | tf_op jit(solution)/shard_map/gather | solution.py:48
  444.0 3.0 fusion.6
  447.0 0.8 copy.42
  447.8 1.7 fusion.4
  449.5 0.7 copy.34
  450.2 78.9 %all-to-all-done.3 = bf16[64,20,1536]{2,1,0:T(8,128)(2,1)} async-done(((bf16[64,20,1536]{2,1,0:T(8,128)(2,1)}), bf16[64,20,1536]{2,1,0:T(8,128)(2,1)}, u32[]{:S(2)}, u32[]{:S(2)}) %all-to-all-start.3) | async-done | bytes 3932192 | tf_op jit(solution)/shard_map/all_to_all | solution.py:71
  529.0 6.9 %reshape.110 = bf16[1280,1536]{1,0:T(8,128)(2,1)} reshape(bf16[64,20,1536]{2,1,0:T(8,128)(2,1)} %all-to-all-done.3) | data formatting | bytes 7864320 | tf_op jit(solution)/shard_map/reshape | solution.py:78
  535.9 10.0 %gather_fusion.1 = bf16[1024,1536]{1,0:T(8,128)(2,1)} fusion(bf16[1280,1536]{1,0:T(8,128)(2,1)} %reshape.110, s32[1024]{0:T(1024)S(1)} %broadcast_clamp_fusion), kind=kCustom, calls=%fused_computation.1 | custom fusion | bytes 6295552 | tf_op jit(solution)/shard_map/gather | solution.py:78
  545.9 4.7 bitcast_reduce_fusion
  (44 shorter events, 1.2 us)
Async XLA Ops:
  7.2 276.3 %copy-start = (bf16[1,384,1536]{2,1,0:T(8,128)(2,1)S(1)}, bf16[1,384,1536]{2,1,0:T(8,128)(2,1)}, u32[]{:S(2)}) copy-start(bf16[1,384,1536]{2,1,0:T(8,128)(2,1)} %param.13) | copy-start | bytes 3538948
  42.8 13.5 %copy-start.11 = (f32[128,8]{0,1:T(8,128)S(1)}, f32[128,8]{0,1:T(8,128)}, u32[]{:S(2)}) copy-start(f32[128,8]{0,1:T(8,128)} %param.9) | copy-start | bytes 12292
  42.8 13.7 %copy-start.9 = (bf16[128,1536]{1,0:T(8,128)(2,1)S(1)}, bf16[128,1536]{1,0:T(8,128)(2,1)}, u32[]{:S(2)}) copy-start(bf16[128,1536]{1,0:T(8,128)(2,1)} %param.10) | copy-start | bytes 1179652
  42.8 120.6 %all-to-all-start = ((bf16[64,20,1536]{2,1,0:T(8,128)(2,1)}), bf16[64,20,1536]{2,1,0:T(8,128)(2,1)}, u32[]{:S(2)}, u32[]{:S(2)}) async-start(bf16[64,20,1536]{2,1,0:T(8,128)(2,1)} %reshape.102), calls=%async_computation | async-start | bytes 9437184 | tf_op jit(solution)/shard_map/all_to_all | solution.py:23
  163.4 113.2 %all-to-all-start.2 = ((bf16[64,20,1536]{2,1,0:T(8,128)(2,1)}), bf16[64,20,1536]{2,1,0:T(8,128)(2,1)}, u32[]{:S(2)}, u32[]{:S(2)}) async-start(bf16[64,20,1536]{2,1,0:T(8,128)(2,1)} %reshape.107), calls=%async_computation.2 | async-start | bytes 9437184 | tf_op jit(solution)/shard_map/all_to_all | solution.py:47
  176.3 6.1 %copy-start.3 = (bf16[1280,1536]{1,0:T(8,128)(2,1)S(1)}, bf16[1280,1536]{1,0:T(8,128)(2,1)}, u32[]{:S(2)}) copy-start(bf16[1280,1536]{1,0:T(8,128)(2,1)} %reshape.103) | copy-start | bytes 11796484
  176.3 6.1 %copy-start.5 = (bf16[1,1536,384]{2,1,0:T(8,128)(2,1)S(1)}, bf16[1,1536,384]{2,1,0:T(8,128)(2,1)}, u32[]{:S(2)}) copy-start(bf16[1,1536,384]{2,1,0:T(8,128)(2,1)} %param.11) | copy-start | bytes 3538948
  290.7 0.9 copy-start.12
  302.5 113.2 %all-to-all-start.1 = ((bf16[64,20,1536]{2,1,0:T(8,128)(2,1)}), bf16[64,20,1536]{2,1,0:T(8,128)(2,1)}, u32[]{:S(2)}, u32[]{:S(2)}) async-start(bf16[64,20,1536]{2,1,0:T(8,128)(2,1)} %reshape.104), calls=%async_computation.1 | async-start | bytes 9437184 | tf_op jit(solution)/shard_map/all_to_all | solution.py:46
  308.5 113.7 %reduce-scatter.4.cloned.1.call-start = ((), (), s32[]{:S(2)}) async-start(), calls=%async_computation.5 | async-start | bytes 4423680
  308.8 4.3 copy-start.4
  308.8 4.3 copy-start.7
  324.4 2.3 copy-start.6
  324.5 2.3 copy-start.8
  415.7 113.4 %all-to-all-start.3 = ((bf16[64,20,1536]{2,1,0:T(8,128)(2,1)}), bf16[64,20,1536]{2,1,0:T(8,128)(2,1)}, u32[]{:S(2)}, u32[]{:S(2)}) async-start(bf16[64,20,1536]{2,1,0:T(8,128)(2,1)} %reshape.109), calls=%async_computation.3 | async-start | bytes 9437184 | tf_op jit(solution)/shard_map/all_to_all | solution.py:71
  444.0 3.8 copy-start.2
  444.0 3.8 copy-start.10
  535.9 14.7 %copy-start.1 = (bf16[1,384,1536]{2,1,0:T(8,128)(2,1)S(1)}, bf16[1,384,1536]{2,1,0:T(8,128)(2,1)}, u32[]{:S(2)}) copy-start(bf16[1,384,1536]{2,1,0:T(8,128)(2,1)} %param.13) | copy-start | bytes 3538948
Sparse Core Ops, SparseCore 0:
  324.6 44.9 reduce-scatter.3
where the time goes:
time: 568 us; the launch traced here: 558 us
  waiting for transfers between devices  339 us (60%)
  local copies, waits for them, and re-layouts  97.8 us (17%)
  matrix products  39.9 us (7%)
  other arithmetic  34.4 us (6%)
  starting transfers between devices  32.1 us (6%)
  between operations  14.5 us (3%)
    all_to_all x1, waiting for transfers between devices, shards(): lax.all_to_all(outgoing.reshape(experts, capacity, model_width), 'expert'...  91.7 us
    all_to_all x1, waiting for transfers between devices, shards(): lax.all_to_all(grad_blocks, 'expert', split_axis=0, concat_axis=0, tiled=...  90.5 us
    all_to_all x1, waiting for transfers between devices, shards(): lax.all_to_all(grad_route.reshape(experts, capacity, model_width), 'exper...  78.9 us
    all_to_all x1, waiting for transfers between devices, shards(): lax.all_to_all(out_blocks, 'expert', split_axis=0, concat_axis=0, tiled=T...  78 us
    another operation x3, other arithmetic  18.2 us
    all_to_all x1, starting transfers between devices, shards(): lax.all_to_all(outgoing.reshape(experts, capacity, model_width), 'expert'...  13.5 us
    unnamed x33, local copies, waits for them, and re-layouts  11.7 us
  transfers between devices with their start and end apart: 5, of which 4 were waited for; matrix products, arithmetic and copies ran while one was open for 16% of the time, Pallas kernels for 0%

commit v1 on v0

v1 whole, which is shorter than its diff:
```python
import jax
import jax.numpy as jnp
from jax import lax
from jax.experimental import pallas as pl
from jax.experimental.pallas import tpu as pltpu
from jax.sharding import PartitionSpec as P

MESH = pl.DeviceIdType.MESH
F32 = jnp.float32
BF16 = jnp.bfloat16
NX, NY, NZ, NJ = 4, 4, 8, 8
T = 128
CAP = 20
Q = 4
DQ = 384
BLK = Q * CAP
R = NJ * BLK
TQ = Q * T
F = 384
D = 1536
ROWS = NJ * CAP
BATCH = 2 * ROWS
WROWS = F + F // 2


def dot(a, b):
    return jnp.dot(a, b, preferred_element_type=F32)


def dot_nt(a, b):
    return lax.dot_general(a, b, (((1,), (1,)), ((), ())), preferred_element_type=F32)


def dot_tn(a, b):
    return lax.dot_general(a, b, (((0,), (0,)), ((), ())), preferred_element_type=F32)


def dot_f32(a, b):
    return jnp.dot(a, b, preferred_element_type=F32, precision=lax.Precision.HIGHEST)


def iota(shape, dim):
    return lax.broadcasted_iota(jnp.int32, shape, dim)


def div20(v):
    return (v * 3277) >> 16


def wait(ref, sem):
    pltpu.make_async_copy(ref, ref, sem).wait()


def kernel(
    routes_ref, probs_ref, tok_ref, cot_ref, wg_hbm, wu_hbm, wd_hbm,
    out_ref, gtok_ref, gprob_ref, ogate_ref, oup_ref, odown_ref,
    wg, wu, wd, held, sent, rows_in, rows_back, xs, ss, hid, zback, wpart, perm, perm_t, psum,
    meta, meta_in, gs, gp_a, gp_b, gp_c, gp_d,
    w_sem, z_send, z_recv, m_send, m_recv, y_send, y_recv, r_send, r_recv,
    b_send, b_recv, x_send, x_recv, g_send, g_recv,
):
    mx = lax.axis_index("mirror")
    e = lax.axis_index("expert")
    y, z, core = e // 16, (e // 2) % 8, e % 2
    j = y * 2 + core

    def dev_j(other):
        return (mx, (other // 2) * 16 + z * 2 + other % 2)

    def dev_z(step):
        return (mx, y * 16 + ((z + step + 8) % 8) * 2 + core)

    def dev_x(step):
        return ((mx + step) % 4, e)

    offsets = [0, -1, 1, -2, 2, -3, 3, -4]

    barrier = pltpu.get_barrier_semaphore()
    for k in range(1, 8):
        pl.semaphore_signal(barrier, inc=1, device_id=dev_j((j + k) % 8), device_id_type=MESH)
        pl.semaphore_signal(barrier, inc=1, device_id=dev_z(k), device_id_type=MESH)
    for k in range(1, 4):
        pl.semaphore_signal(barrier, inc=1, device_id=dev_x(k), device_id_type=MESH)

    weights = [
        pltpu.make_async_copy(src, dst, w_sem.at[n])
        for n, (src, dst) in enumerate(((wg_hbm, wg), (wu_hbm, wu), (wd_hbm, wd)))
    ]
    for copy in weights:
        copy.start()

    for q in range(Q):
        held[0, 0, q * T : (q + 1) * T, :] = tok_ref[:, q * DQ : (q + 1) * DQ]
        held[0, 1, q * T : (q + 1) * T, :] = cot_ref[:, q * DQ : (q + 1) * DQ]

    row = iota((64, T), 0)
    expert = (((row & 7) >> 1) << 4) + ((row >> 3) << 1) + (row & 1)
    member = jnp.zeros((64, T), F32)
    weight = jnp.zeros((64, T), F32)
    for k in range(8):
        hit = routes_ref[k : k + 1, :] == expert
        member = member + jnp.where(hit, 1.0, 0.0)
        weight = weight + jnp.where(hit, probs_ref[k : k + 1, :], 0.0)
    before = jnp.where(iota((T, T), 0) < iota((T, T), 1), 1.0, 0.0).astype(BF16)
    rank = dot(member.astype(BF16), before)
    code = jnp.where(member > 0.5, rank, -1.0)
    for p in range(NZ):
        meta[p, 0:8, :] = code[p * 8 : (p + 1) * 8, :]
        meta[p, 8:16, :] = weight[p * 8 : (p + 1) * 8, :]
    meta_in[0] = meta[z]

    pl.semaphore_wait(barrier, 17)

    def remote(src, dst, send, recv, device):
        return pltpu.make_async_remote_copy(
            src_ref=src, dst_ref=dst, send_sem=send, recv_sem=recv, device_id=device, device_id_type=MESH
        )

    for a in range(2):
        for slot, step in ((1, 1), (2, -1)):
            remote(held.at[0, a], held.at[slot, a], z_send.at[0], z_recv.at[slot, a], dev_z(step)).start()
        if a == 0:
            for i in range(1, 8):
                to = -offsets[i]
                remote(
                    meta.at[(z + to + 8) % 8], meta_in.at[i], m_send.at[i], m_recv.at[i], dev_z(to)
                ).start()

    lane = iota((R, R), 1)
    r = iota((R, R), 0)
    r20 = div20(r)
    slot_of = r - r20 * 20
    perm[...] = jnp.where(lane == (r20 & 7) * BLK + (r20 >> 3) * CAP + slot_of, 1.0, 0.0).astype(BF16)
    perm_t[...] = jnp.where(
        lane == (r20 & 3) * ROWS + (r20 >> 2) * CAP + slot_of, 1.0, 0.0
    ).astype(BF16)

    r80 = iota((BLK, T), 0)
    q80 = div20(r80)
    slot80 = (r80 - q80 * CAP).astype(F32)

    def select(i, weighted):
        tops, lows = [], []
        for n in range(NJ):
            hit = meta_in[i, n : n + 1, :] == slot80
            if weighted:
                value = jnp.where(hit, meta_in[i, 8 + n : 9 + n, :], 0.0)
            else:
                value = jnp.where(hit, 1.0, 0.0)
            parts = [jnp.where(q80 == q, value, 0.0) for q in range(Q)]
            block = jnp.concatenate(parts, axis=1)
            top = block.astype(BF16)
            tops.append(top)
            if weighted:
                lows.append((block - top.astype(F32)).astype(BF16))
        top = jnp.concatenate(tops, axis=0)
        return (top, jnp.concatenate(lows, axis=0)) if weighted else (top,)

    def unit(i, a):
        s = i % 4

        @pl.when(i >= 1)
        def _():
            wait(held.at[i, a], z_recv.at[i, a])

        @pl.when((i >= 1) & (i <= 4))
        def _():
            step = 2 * (i % 2) - 1
            remote(held.at[i, a], held.at[i + 2, a], z_send.at[i], z_recv.at[i + 2, a], dev_z(step)).start()

        @pl.when(i == 5)
        def _():
            half = held.at[5, a, pl.ds(0, 256)]
            remote(half, held.at[7, a, pl.ds(0, 256)], z_send.at[5], z_recv.at[7, a], dev_z(1)).start()

        @pl.when(i == 6)
        def _():
            half = held.at[6, a, pl.ds(256, 256)]
            remote(half, held.at[7, a, pl.ds(256, 256)], z_send.at[6], z_recv.at[7, a], dev_z(-1)).start()

        if a == 0:

            @pl.when(i >= 1)
            def _():
                wait(meta_in.at[i], m_recv.at[i])

        source = held[i, a]
        picked = sum(dot(m, source) for m in select(i, a == 1))

        @pl.when(i >= 4)
        def _():
            wait(sent.at[s, a, pl.ds(0, 7 * BLK)], y_send.at[s, a])

        sent[s, a] = picked.astype(BF16)
        mine = pl.ds(pl.multiple_of(j * BLK, 16), BLK)
        rows_in[i, a, mine, :] = sent[s, a, mine, :]

        def send(k, _):
            other = (j + k) % 8
            theirs = pl.ds(pl.multiple_of(other * BLK, 16), BLK)
            remote(
                sent.at[s, a, theirs], rows_in.at[i, a, mine], y_send.at[s, a], y_recv.at[i], dev_j(other)
            ).start()
            return 0

        lax.fori_loop(1, 8, send, 0)

    def compute(c):
        base = pl.multiple_of(c * BATCH, 16)
        slots = (2 * c + 1, (2 * c + 2) % 8)
        for m, i in enumerate(slots):
            wait(rows_in.at[i, :, pl.ds(0, 7 * BLK)], y_recv.at[i])
            for a, store in ((0, xs), (1, ss)):
                flat = dot(perm[...], rows_in[i, a]).astype(BF16)
                for q in range(Q):
                    store[pl.ds(base + m * ROWS, ROWS), q * DQ : (q + 1) * DQ] = flat[
                        q * ROWS : (q + 1) * ROWS, :
                    ]
        batch = pl.ds(base, BATCH)
        x = xs[batch, :]
        pre_gate = dot(x, wg[...])
        pre_up = dot(x, wu[...])
        sig = jax.nn.sigmoid(pre_gate)
        hidden = (pre_gate * sig * pre_up).astype(BF16)
        grad_hidden = dot_nt(ss[batch, :], wd[...])
        grad_gate = (grad_hidden * pre_up * sig * (1.0 + pre_gate * (1.0 - sig))).astype(BF16)
        grad_up = (grad_hidden * pre_gate * sig).astype(BF16)
        hid[0, batch, :] = grad_gate
        hid[1, batch, :] = grad_up
        hid[2, batch, :] = hidden
        total = jnp.sum(grad_hidden * hidden.astype(F32), axis=1, keepdims=True)
        gs[batch, :] = jnp.broadcast_to(total, (BATCH, 128))
        out = dot(hidden, wd[...]).astype(BF16)
        for m, i in enumerate(slots):
            part = out[m * ROWS : (m + 1) * ROWS, :]
            flat = jnp.concatenate([part[:, q * DQ : (q + 1) * DQ] for q in range(Q)], axis=0)
            rows_in[i, 0] = dot(perm_t[...], flat).astype(BF16)
        grad = (dot_nt(grad_gate, wg[...]) + dot_nt(grad_up, wu[...])).astype(BF16)
        for m, i in enumerate(slots):
            part = grad[m * ROWS : (m + 1) * ROWS, :]
            flat = jnp.concatenate([part[:, q * DQ : (q + 1) * DQ] for q in range(Q)], axis=0)
            rows_in[i, 1] = dot(perm_t[...], flat).astype(BF16)

    def give_back(i):
        mine = pl.ds(pl.multiple_of(j * BLK, 16), BLK)
        for a in range(2):
            rows_back[i, a, mine, :] = rows_in[i, a, mine, :]

        def send(k, _):
            other = (j + k) % 8
            theirs = pl.ds(pl.multiple_of(other * BLK, 16), BLK)
            for a in range(2):
                remote(
                    rows_in.at[i, a, theirs], rows_back.at[i, a, mine], r_send.at[i], r_recv.at[i], dev_j(other)
                ).start()
            return 0

        lax.fori_loop(1, 8, send, 0)

    def group(g, _):
        first = jnp.minimum(jnp.maximum(2 * g - 1, 0), 8)
        last = jnp.minimum(2 * g + 1, 8)
        for a in range(2):

            def one(i, _, a=a):
                unit(i, a)
                return 0

            lax.fori_loop(first, last, one, 0)

        @pl.when(g == 2)
        def _():
            for copy in weights:
                copy.wait()

        @pl.when(g >= 2)
        def _():
            compute(g - 2)

        @pl.when(g == 4)
        def _():
            give_back(6)
            give_back(5)

        @pl.when(g == 5)
        def _():
            give_back(7)

        return 0

    lax.fori_loop(0, 6, group, 0)

    row = iota((8 * ROWS, 128), 0)
    lanes = iota((8 * ROWS, 128), 1)
    spread = jnp.where(lanes == row - div20(row) * CAP, gs[...], 0.0)
    row = iota((64, 8 * ROWS), 0)
    block = div20(iota((64, 8 * ROWS), 1))
    pick = jnp.where(row == (block & 7) * 8 + (((block >> 3) + 1) & 7), 1.0, 0.0)
    gp_a[...] = dot_f32(pick, spread)
    tile = pl.ds(pl.multiple_of(j * 8, 8), 8)
    gp_b[tile, :] = gp_a[tile, :]

    def send_gp(k, _):
        other = (j + k) % 8
        theirs = pl.ds(pl.multiple_of(other * 8, 8), 8)
        remote(gp_a.at[theirs], gp_b.at[tile], g_send.at[0], g_recv.at[0], dev_j(other)).start()
        return 0

    lax.fori_loop(1, 8, send_gp, 0)

    for s in range(4):
        for a in range(2):
            wait(sent.at[s, a, pl.ds(0, 7 * BLK)], y_send.at[s, a])

    def grads(n, _):
        for kind, store in ((0, xs), (1, xs), (2, ss)):
            cols = pl.ds(pl.multiple_of(n * DQ, 128), DQ)
            part = dot_tn(hid[kind], store[:, cols]).astype(BF16)
            if kind == 0:
                sent[n, 0, 0:F, :] = part
            elif kind == 1:
                sent[n, 1, 0:F, :] = part
            else:
                sent[n, 0, F:WROWS, :] = part[0 : F // 2, :]
                sent[n, 1, F:WROWS, :] = part[F // 2 :, :]
        return 0

    lax.fori_loop(0, 4, grads, 0)
    for k in range(1, 4):
        other = (mx + k) % 4
        remote(
            sent.at[other, :, pl.ds(0, WROWS)],
            wpart.at[k - 1],
            x_send.at[k - 1],
            x_recv.at[k - 1],
            dev_x(k),
        ).start()

    def back(t, _):
        i = 7 - t

        @pl.when(i >= 3)
        def _():
            give_back(i - 3)

        wait(rows_back.at[i, :, pl.ds(0, 7 * BLK)], r_recv.at[i])
        weighted = select(i, True)
        psum[0] = sum(dot_tn(m, rows_back[i, 0]) for m in weighted)
        psum[1] = dot_tn(select(i, False)[0], rows_back[i, 1])

        @pl.when((i >= 1) & (i <= 4))
        def _():
            wait(zback.at[i + 2], b_recv.at[i + 2])
            psum[...] = psum[...] + zback[i + 2].astype(F32)

        @pl.when(i == 5)
        def _():
            wait(zback.at[7, :, pl.ds(0, 256)], b_recv.at[0])
            psum[:, 0:256, :] = psum[:, 0:256, :] + zback[7, :, 0:256, :].astype(F32)

        @pl.when(i == 6)
        def _():
            wait(zback.at[7, :, pl.ds(256, 256)], b_recv.at[7])
            psum[:, 256:512, :] = psum[:, 256:512, :] + zback[7, :, 256:512, :].astype(F32)

        @pl.when((i >= 1) & (i <= 4))
        def _():
            wait(held.at[i], z_send.at[i])

        @pl.when((i >= 5) & (i <= 6))
        def _():
            wait(held.at[i, :, pl.ds(0, 256)], z_send.at[i])

        @pl.when(i >= 1)
        def _():
            held[i] = psum[...].astype(BF16)

        @pl.when((i >= 1) & (i <= 6))
        def _():
            step = 1 - 2 * (i % 2)
            remote(held.at[i], zback.at[i], b_send.at[i], b_recv.at[i], dev_z(step)).start()

        @pl.when(i == 7)
        def _():
            for lo, step, n in ((0, -1, 0), (256, 1, 7)):
                half = (7, slice(None), pl.ds(lo, 256))
                remote(held.at[half], zback.at[half], b_send.at[n], b_recv.at[n], dev_z(step)).start()

        @pl.when(i == 6)
        def _():
            wait(gp_b.at[pl.ds(0, 56)], g_recv.at[0])
            row = iota((64, 64), 0)
            col = iota((64, 64), 1)
            turn = jnp.where(col == (row & 7) * 8 + (row >> 3), 1.0, 0.0)
            gp_c[...] = dot_f32(turn, gp_b[...])
            own = pl.ds(pl.multiple_of(z * 8, 8), 8)
            gp_d[own, :] = gp_c[0:8, :]
            for i in range(1, 8):
                remote(
                    gp_c.at[pl.ds(i * 8, 8)], gp_d.at[own], g_send.at[1], g_recv.at[1], dev_z(offsets[i])
                ).start()

        @pl.when(i == 3)
        def _():
            wait(gp_d.at[pl.ds(0, 56)], g_recv.at[1])
            row = iota((64, T), 0)
            expert = (((row & 7) >> 1) << 4) + ((row >> 3) << 1) + (row & 1)
            code = jnp.concatenate([meta[p, 0:8, :] for p in range(NZ)], axis=0)
            dense = jnp.zeros((64, T), F32)
            values = gp_d[...]
            for n in range(CAP):
                dense = dense + jnp.where(code == float(n), values[:, n : n + 1], 0.0)
            for k in range(8):
                hit = routes_ref[k : k + 1, :] == expert
                found = jnp.sum(jnp.where(hit, dense, 0.0), axis=0, keepdims=True)
                gprob_ref[k : k + 1, :] = found / probs_ref[k : k + 1, :]

        @pl.when(i == 2)
        def _():
            for n in range(3):
                wait(wpart.at[n], x_recv.at[n])
            mine = sent[mx, :, 0:WROWS, :].astype(F32)
            total = ((mine + wpart[0].astype(F32)) + wpart[1].astype(F32)) + wpart[2].astype(F32)
            ogate_ref[...] = jnp.transpose(total[0, 0:F])
            oup_ref[...] = jnp.transpose(total[1, 0:F])
            odown_ref[0 : F // 2, :] = total[0, F:WROWS]
            odown_ref[F // 2 :, :] = total[1, F:WROWS]

        return 0

    lax.fori_loop(0, 8, back, 0)

    for n in (1, 2):
        wait(zback.at[n], b_recv.at[n])
    for a, ref in ((0, out_ref), (1, gtok_ref)):
        total = psum[a] + zback[1, a].astype(F32) + zback[2, a].astype(F32)
        for q in range(Q):
            ref[:, q * DQ : (q + 1) * DQ] = total[q * T : (q + 1) * T, :].astype(BF16)

    wait(held.at[pl.ds(0, 2)], z_send.at[0])
    for i in range(1, 8):
        wait(meta.at[0], m_send.at[i])
    for i in range(8):
        wait(rows_in.at[i, :, pl.ds(0, 7 * BLK)], r_send.at[i])
    for i in range(1, 7):
        wait(held.at[i], b_send.at[i])
    for lo, n in ((0, 0), (256, 7)):
        wait(held.at[7, :, pl.ds(lo, 256)], b_send.at[n])
    for n in range(3):
        wait(wpart.at[n], x_send.at[n])
    for n in range(2):
        wait(gp_b.at[pl.ds(0, 56)], g_send.at[n])


def shards(tokens, routes, gate_probs, cotangent, w_gate, w_up, w_down):
    vmem = pl.BlockSpec(memory_space=pltpu.VMEM)
    hbm = pl.BlockSpec(memory_space=pl.ANY)
    dma = pltpu.SemaphoreType.DMA
    out, gtok, gprob, ogate, oup, odown = pl.pallas_call(
        kernel,
        out_shape=(
            jax.ShapeDtypeStruct((T, D), BF16),
            jax.ShapeDtypeStruct((T, D), BF16),
            jax.ShapeDtypeStruct((8, T), F32),
            jax.ShapeDtypeStruct((F, F), F32),
            jax.ShapeDtypeStruct((F, F), F32),
            jax.ShapeDtypeStruct((F, F), F32),
        ),
        in_specs=[vmem] * 4 + [hbm] * 3,
        out_specs=(vmem,) * 6,
        scratch_shapes=[
            pltpu.VMEM((D, F), BF16),
            pltpu.VMEM((D, F), BF16),
            pltpu.VMEM((F, D), BF16),
            pltpu.VMEM((8, 2, TQ, DQ), BF16),
            pltpu.VMEM((4, 2, R, DQ), BF16),
            pltpu.VMEM((8, 2, R, DQ), BF16),
            pltpu.VMEM((8, 2, R, DQ), BF16),
            pltpu.VMEM((8 * ROWS, D), BF16),
            pltpu.VMEM((8 * ROWS, D), BF16),
            pltpu.VMEM((3, 8 * ROWS, F), BF16),
            pltpu.VMEM((8, 2, TQ, DQ), BF16),
            pltpu.VMEM((3, 2, WROWS, DQ), BF16),
            pltpu.VMEM((R, R), BF16),
            pltpu.VMEM((R, R), BF16),
            pltpu.VMEM((2, TQ, DQ), F32),
            pltpu.VMEM((8, 16, T), F32),
            pltpu.VMEM((8, 16, T), F32),
            pltpu.VMEM((8 * ROWS, 128), F32),
            pltpu.VMEM((64, 128), F32),
            pltpu.VMEM((64, 128), F32),
            pltpu.VMEM((64, 128), F32),
            pltpu.VMEM((64, 128), F32),
            dma((3,)),
            dma((7,)),
            dma((8, 2)),
            dma((8,)),
            dma((8,)),
            dma((4, 2)),
            dma((8,)),
            dma((8,)),
            dma((8,)),
            dma((8,)),
            dma((8,)),
            dma((3,)),
            dma((3,)),
            dma((2,)),
            dma((2,)),
        ],
        compiler_params=pltpu.CompilerParams(
            collective_id=0, has_side_effects=True, vmem_limit_bytes=63 * 2**20
        ),
        cost_estimate=pl.CostEstimate(flops=20 * 10**9, bytes_accessed=10**7, transcendentals=10**6),
    )(routes.T, gate_probs.T, tokens, cotangent, w_gate[0], w_up[0], w_down[0])
    return (out, gtok, gprob.T, ogate[None], oup[None], odown[None])


def solution(mesh):
    placed = (
        P(("mirror", "expert"), None),
        P(("mirror", "expert"), None),
        P(("mirror", "expert"), None),
        P(("mirror", "expert"), None),
        P("expert", None, None),
        P("expert", None, None),
        P("expert", None, None),
    )
    return jax.shard_map(
        shards,
        mesh=mesh,
        in_specs=placed,
        out_specs=(
            P(("mirror", "expert"), None),
            P(("mirror", "expert"), None),
            P(("mirror", "expert"), None),
            P("expert", "mirror", None),
            P("expert", "mirror", None),
            P("expert", None, "mirror"),
        ),
        check_vma=False,
    )
```

time: 568 us -> 208 us (0.37); the launches traced: 558 us -> 208 us
  waiting for transfers between devices: 339 us -> 0 us
  Pallas kernels: 0 us -> 201 us
  local copies, waits for them, and re-layouts: 97.8 us -> 6.71 us
  matrix products: 39.9 us -> 0 us
  other arithmetic: 34.4 us -> 0 us
  starting transfers between devices: 32.1 us -> 0 us
  between operations: 14.5 us -> 0.66 us
    all_to_all x4 -> x0, waiting for transfers between devices: 339 us -> none  [the longest x1 91.7 us: shards(): lax.all_to_all(outgoing.reshape(experts, capacity, model_width), 'expert'...]
    pallas_call x0 -> x1, Pallas kernels: none -> 201 us  [shards(): pl.pallas_call(kernel, out_shape=(jax.ShapeDtypeStruct((T, D), BF16), jax...]
    reshape x8 -> x0, local copies, waits for them, and re-layouts: 54.7 us -> none  [the longest x1 6.89 us: shards(): scaled_rows = grad_arrived.reshape(slot_total, model_width)]
    dot_general x11 -> x0, matrix products: 39.9 us -> none  [the longest x1 7.21 us: shards(): lax.dot_general(scaled_rows, down_mat, (((1,), (1,)), ((), ())), preferre...]
    all_to_all x4 -> x0, starting transfers between devices: 31.9 us -> none  [the longest x1 13.5 us: shards(): lax.all_to_all(outgoing.reshape(experts, capacity, model_width), 'expert'...]
    gather x2 -> x0, local copies, waits for them, and re-layouts: 19.9 us -> none  [the longest x1 9.99 us: shards(): grad_back.reshape(slot_total, model_width)[destination]]
    another operation x3 -> x0, other arithmetic: 18.2 us -> none
    scatter x1 -> x0, other arithmetic: 8.31 us -> none  [shards(): jnp.zeros((slot_total, model_width), jnp.bfloat16).at[destination]]
  transfers between devices with their start and end apart: 5 -> 0, of which waited for: 4 -> 0; matrix products, arithmetic and copies ran while one was open for 16% -> 0% of each run, Pallas kernels for 0% -> 0%
where the time goes in v1:
time: 208 us
  Pallas kernels  201 us (97%)
  local copies, waits for them, and re-layouts  6.71 us (3%)
    pallas_call x1, Pallas kernels, shards(): pl.pallas_call(kernel, out_shape=(jax.ShapeDtypeStruct((T, D), BF16), jax...  201 us
    unnamed x14, local copies, waits for them, and re-layouts  6.71 us

profile of v1, /device:TPU:1, one launch (start us, length us, event | category | flops | bytes accessed | tf_op | source)
XLA Modules:
  0.0 208.2 jit_solution(5517921703477633589)
XLA Ops:
  0.6 200.8 %shard_map.118 = (bf16[128,1536]{1,0:T(8,128)(2,1)}, bf16[128,1536]{1,0:T(8,128)(2,1)}, f32[8,128]{1,0:T(8,128)}, f32[384,384]{1,0:T(8,128)}, f32[384,384]{1,0:T(8,128)}, /*index=5*/f32[384,384]{1,0:T(8,128)}) custom-call(s32[8,128]{1,0:T(8,128)} %bitcast.16, f32[8,128]{1,0:T(8,128)} %bitcast.17, bf16[128,1536]{1,0:T(8,128)(2,1)} %tok_ref.1, ...), custom_call_target="tpu_custom_call" | custom-call | flops 20000000000 | bytes 10000000 | tf_op jit(solution)/shard_map/pallas_call | solution.py:459
  201.4 0.0 copy-start.3
  201.4 0.0 copy-start.2
  201.4 1.8 copy.19
  203.3 0.0 copy-start.1
  203.3 1.8 copy.20
  205.1 0.0 copy-done.3
  205.1 0.6 copy.21
  205.7 0.0 copy-done.2
  205.7 0.0 copy-start
  205.7 0.8 copy.22
  206.5 0.0 copy-done.1
  206.5 0.8 copy.23
  207.3 0.0 copy-done
  207.3 0.8 copy.24
Async XLA Ops:
  201.4 3.7 %copy-start.3 = (f32[8,128]{1,0:T(8,128)S(1)}, f32[8,128]{1,0:T(8,128)}, u32[]{:S(2)}) copy-start(f32[8,128]{1,0:T(8,128)} %get-tuple-element.14) | copy-start | bytes 12292
  201.4 4.3 %copy-start.2 = (f32[384,384]{1,0:T(8,128)S(1)}, f32[384,384]{1,0:T(8,128)}, u32[]{:S(2)}) copy-start(f32[384,384]{1,0:T(8,128)} %get-tuple-element.15) | copy-start | bytes 1769476
  203.3 3.2 %copy-start.1 = (f32[384,384]{1,0:T(8,128)S(1)}, f32[384,384]{1,0:T(8,128)}, u32[]{:S(2)}) copy-start(f32[384,384]{1,0:T(8,128)} %get-tuple-element.16) | copy-start | bytes 1769476
  205.7 1.6 copy-start

commit v2 on v1

--- a/solution.py
+++ b/solution.py
@@ -125,15 +125,6 @@
                 remote(
                     meta.at[(z + to + 8) % 8], meta_in.at[i], m_send.at[i], m_recv.at[i], dev_z(to)
                 ).start()
-
-    lane = iota((R, R), 1)
-    r = iota((R, R), 0)
-    r20 = div20(r)
-    slot_of = r - r20 * 20
-    perm[...] = jnp.where(lane == (r20 & 7) * BLK + (r20 >> 3) * CAP + slot_of, 1.0, 0.0).astype(BF16)
-    perm_t[...] = jnp.where(
-        lane == (r20 & 3) * ROWS + (r20 >> 2) * CAP + slot_of, 1.0, 0.0
-    ).astype(BF16)
 
     r80 = iota((BLK, T), 0)
     q80 = div20(r80)
@@ -241,25 +232,46 @@
             flat = jnp.concatenate([part[:, q * DQ : (q + 1) * DQ] for q in range(Q)], axis=0)
             rows_in[i, 1] = dot(perm_t[...], flat).astype(BF16)
 
-    def give_back(i):
+    def give_back(i, a):
         mine = pl.ds(pl.multiple_of(j * BLK, 16), BLK)
-        for a in range(2):
-            rows_back[i, a, mine, :] = rows_in[i, a, mine, :]
+        rows_back[i, a, mine, :] = rows_in[i, a, mine, :]
 
         def send(k, _):
             other = (j + k) % 8
             theirs = pl.ds(pl.multiple_of(other * BLK, 16), BLK)
-            for a in range(2):
-                remote(
-                    rows_in.at[i, a, theirs], rows_back.at[i, a, mine], r_send.at[i], r_recv.at[i], dev_j(other)
-                ).start()
+            remote(
+                rows_in.at[i, a, theirs], rows_back.at[i, a, mine], r_send.at[i], r_recv.at[i, a], dev_j(other)
+            ).start()
             return 0
 
         lax.fori_loop(1, 8, send, 0)
 
+    def give_group(g):
+        first, last = bounds(g)
+        for a in range(2):
+
+            def one(i, _, a=a):
+                give_back(i, a)
+                return 0
+
+            lax.fori_loop(first, last, one, 0)
+
+    def bounds(g):
+        return jnp.minimum(jnp.maximum(2 * g - 1, 0), 8), jnp.minimum(2 * g + 1, 8)
+
+    def make_perms():
+        lane = iota((R, R), 1)
+        r = iota((R, R), 0)
+        r20 = div20(r)
+        slot_of = r - r20 * 20
+        perm[...] = jnp.where(lane == (r20 & 7) * BLK + (r20 >> 3) * CAP + slot_of, 1.0, 0.0).astype(BF16)
+        perm_t[...] = jnp.where(
+            lane == (r20 & 3) * ROWS + (r20 >> 2) * CAP + slot_of, 1.0, 0.0
+        ).astype(BF16)
+
+
     def group(g, _):
-        first = jnp.minimum(jnp.maximum(2 * g - 1, 0), 8)
-        last = jnp.minimum(2 * g + 1, 8)
+        first, last = bounds(g)
         for a in range(2):
 
             def one(i, _, a=a):
@@ -268,6 +280,10 @@
 
             lax.fori_loop(first, last, one, 0)
 
+        @pl.when(g == 0)
+        def _():
+            make_perms()
+
         @pl.when(g == 2)
         def _():
             for copy in weights:
@@ -279,12 +295,14 @@
 
         @pl.when(g == 4)
         def _():
-            give_back(6)
-            give_back(5)
+            for a in range(2):
+                give_back(6, a)
 
         @pl.when(g == 5)
         def _():
-            give_back(7)
+            for i in (7, 5):
+                for a in range(2):
+                    give_back(i, a)
 
         return 0
 
@@ -336,57 +354,67 @@
             dev_x(k),
         ).start()
 
+    def back_unit(i, a):
+        wait(rows_back.at[i, a, pl.ds(0, 7 * BLK)], r_recv.at[i, a])
+        psum[a] = sum(dot_tn(m, rows_back[i, a]) for m in select(i, a == 0))
+
+        @pl.when((i >= 1) & (i <= 4))
+        def _():
+            wait(zback.at[i + 2, a], b_recv.at[i + 2, a])
+            psum[a] = psum[a] + zback[i + 2, a].astype(F32)
+
+        @pl.when(i == 5)
+        def _():
+            wait(zback.at[7, a, pl.ds(0, 256)], b_recv.at[0, a])
+            psum[a, 0:256, :] = psum[a, 0:256, :] + zback[7, a, 0:256, :].astype(F32)
+
+        @pl.when(i == 6)
+        def _():
+            wait(zback.at[7, a, pl.ds(256, 256)], b_recv.at[7, a])
+            psum[a, 256:512, :] = psum[a, 256:512, :] + zback[7, a, 256:512, :].astype(F32)
+
+        if a == 0:
+
+            @pl.when((i >= 1) & (i <= 4))
+            def _():
+                wait(held.at[i], z_send.at[i])
+
+            @pl.when((i >= 5) & (i <= 6))
+            def _():
+                wait(held.at[i, :, pl.ds(0, 256)], z_send.at[i])
+
+        @pl.when(i >= 1)
+        def _():
+            held[i, a] = psum[a].astype(BF16)
+
+        @pl.when((i >= 1) & (i <= 6))
+        def _():
+            step = 1 - 2 * (i % 2)
+            remote(held.at[i, a], zback.at[i, a], b_send.at[i], b_recv.at[i, a], dev_z(step)).start()
+
+        @pl.when(i == 7)
+        def _():
+            for lo, step, n in ((0, -1, 0), (256, 1, 7)):
+                half = (7, a, pl.ds(lo, 256))
+                remote(held.at[half], zback.at[half], b_send.at[n], b_recv.at[n, a], dev_z(step)).start()
+
     def back(t, _):
-        i = 7 - t
-
-        @pl.when(i >= 3)
-        def _():
-            give_back(i - 3)
-
-        wait(rows_back.at[i, :, pl.ds(0, 7 * BLK)], r_recv.at[i])
-        weighted = select(i, True)
-        psum[0] = sum(dot_tn(m, rows_back[i, 0]) for m in weighted)
-        psum[1] = dot_tn(select(i, False)[0], rows_back[i, 1])
-
-        @pl.when((i >= 1) & (i <= 4))
-        def _():
-            wait(zback.at[i + 2], b_recv.at[i + 2])
-            psum[...] = psum[...] + zback[i + 2].astype(F32)
-
-        @pl.when(i == 5)
-        def _():
-            wait(zback.at[7, :, pl.ds(0, 256)], b_recv.at[0])
-            psum[:, 0:256, :] = psum[:, 0:256, :] + zback[7, :, 0:256, :].astype(F32)
-
-        @pl.when(i == 6)
-        def _():
-            wait(zback.at[7, :, pl.ds(256, 256)], b_recv.at[7])
-            psum[:, 256:512, :] = psum[:, 256:512, :] + zback[7, :, 256:512, :].astype(F32)
-
-        @pl.when((i >= 1) & (i <= 4))
-        def _():
-            wait(held.at[i], z_send.at[i])
-
-        @pl.when((i >= 5) & (i <= 6))
-        def _():
-            wait(held.at[i, :, pl.ds(0, 256)], z_send.at[i])
-
-        @pl.when(i >= 1)
-        def _():
-            held[i] = psum[...].astype(BF16)
-
-        @pl.when((i >= 1) & (i <= 6))
-        def _():
-            step = 1 - 2 * (i % 2)
-            remote(held.at[i], zback.at[i], b_send.at[i], b_recv.at[i], dev_z(step)).start()
-
-        @pl.when(i == 7)
-        def _():
-            for lo, step, n in ((0, -1, 0), (256, 1, 7)):
-                half = (7, slice(None), pl.ds(lo, 256))
-                remote(held.at[half], zback.at[half], b_send.at[n], b_recv.at[n], dev_z(step)).start()
-
-        @pl.when(i == 6)
+        g = 4 - t
+        first, last = bounds(g)
+
+        @pl.when((g >= 1) & (g <= 3))
+        def _():
+            give_group(g - 1)
+
+        for a in range(2):
+
+            def one(i, _, a=a):
+                back_unit(i, a)
+                return 0
+
+            lax.fori_loop(first, last, one, 0)
+
+        @pl.when(g == 3)
         def _():
             wait(gp_b.at[pl.ds(0, 56)], g_recv.at[0])
             row = iota((64, 64), 0)
@@ -400,7 +428,7 @@
                     gp_c.at[pl.ds(i * 8, 8)], gp_d.at[own], g_send.at[1], g_recv.at[1], dev_z(offsets[i])
                 ).start()
 
-        @pl.when(i == 3)
+        @pl.when(g == 2)
         def _():
             wait(gp_d.at[pl.ds(0, 56)], g_recv.at[1])
             row = iota((64, T), 0)
@@ -415,7 +443,7 @@
                 found = jnp.sum(jnp.where(hit, dense, 0.0), axis=0, keepdims=True)
                 gprob_ref[k : k + 1, :] = found / probs_ref[k : k + 1, :]
 
-        @pl.when(i == 2)
+        @pl.when(g == 1)
         def _():
             for n in range(3):
                 wait(wpart.at[n], x_recv.at[n])
@@ -428,11 +456,11 @@
 
         return 0
 
-    lax.fori_loop(0, 8, back, 0)
-
-    for n in (1, 2):
-        wait(zback.at[n], b_recv.at[n])
+    lax.fori_loop(0, 5, back, 0)
+
     for a, ref in ((0, out_ref), (1, gtok_ref)):
+        for n in (1, 2):
+            wait(zback.at[n, a], b_recv.at[n, a])
         total = psum[a] + zback[1, a].astype(F32) + zback[2, a].astype(F32)
         for q in range(Q):
             ref[:, q * DQ : (q + 1) * DQ] = total[q * T : (q + 1) * T, :].astype(BF16)
@@ -452,11 +480,24 @@
         wait(gp_b.at[pl.ds(0, 56)], g_send.at[n])
 
 
+def place(*refs):
+    stage, sems = refs[12:18], refs[18]
+    loads = [pltpu.make_async_copy(refs[n], stage[n], sems.at[0, n]) for n in range(6)]
+    stores = [pltpu.make_async_copy(stage[n], refs[n + 6], sems.at[1, n]) for n in range(6)]
+    for copy in loads:
+        copy.start()
+    for load, store in zip(loads, stores):
+        load.wait()
+        store.start()
+    for copy in stores:
+        copy.wait()
+
+
 def shards(tokens, routes, gate_probs, cotangent, w_gate, w_up, w_down):
     vmem = pl.BlockSpec(memory_space=pltpu.VMEM)
     hbm = pl.BlockSpec(memory_space=pl.ANY)
     dma = pltpu.SemaphoreType.DMA
-    out, gtok, gprob, ogate, oup, odown = pl.pallas_call(
+    results = pl.pallas_call(
         kernel,
         out_shape=(
             jax.ShapeDtypeStruct((T, D), BF16),
@@ -499,9 +540,9 @@
             dma((4, 2)),
             dma((8,)),
             dma((8,)),
+            dma((8, 2)),
             dma((8,)),
-            dma((8,)),
-            dma((8,)),
+            dma((8, 2)),
             dma((3,)),
             dma((3,)),
             dma((2,)),
@@ -512,6 +553,13 @@
         ),
         cost_estimate=pl.CostEstimate(flops=20 * 10**9, bytes_accessed=10**7, transcendentals=10**6),
     )(routes.T, gate_probs.T, tokens, cotangent, w_gate[0], w_up[0], w_down[0])
+    out, gtok, gprob, ogate, oup, odown = pl.pallas_call(
+        place,
+        out_shape=tuple(jax.ShapeDtypeStruct(v.shape, v.dtype) for v in results),
+        in_specs=[hbm] * 6,
+        out_specs=(hbm,) * 6,
+        scratch_shapes=[pltpu.VMEM(v.shape, v.dtype) for v in results] + [dma((2, 6))],
+    )(*results)
     return (out, gtok, gprob.T, ogate[None], oup[None], odown[None])
 
 

time: 208 us -> 191 us (0.918)
  Pallas kernels: 201 us -> 190 us
  local copies, waits for them, and re-layouts: 6.71 us -> 0 us
    pallas_call x1, Pallas kernels: 201 us -> 187 us  [shards(): pl.pallas_call(kernel, out_shape=(jax.ShapeDtypeStruct((T, D), BF16), jax...]
    unnamed x14 -> x0, local copies, waits for them, and re-layouts: 6.71 us -> none
    pallas_call x0 -> x1, Pallas kernels: none -> 2.62 us  [shards(): pl.pallas_call(place, out_shape=tuple((jax.ShapeDtypeStruct(v.shape, v.dt...]
where the time goes in v2:
time: 191 us
  Pallas kernels  190 us (99%)
    pallas_call x1, Pallas kernels, shards(): pl.pallas_call(kernel, out_shape=(jax.ShapeDtypeStruct((T, D), BF16), jax...  187 us

profile of v2, /device:TPU:1, one launch (start us, length us, event | category | flops | bytes accessed | tf_op | source)
XLA Modules:
  0.0 190.5 jit_solution(11249038346198353650)
XLA Ops:
  0.6 187.1 %shard_map.118 = (bf16[128,1536]{1,0:T(8,128)(2,1)}, bf16[128,1536]{1,0:T(8,128)(2,1)}, f32[8,128]{1,0:T(8,128)}, f32[384,384]{1,0:T(8,128)}, f32[384,384]{1,0:T(8,128)}, /*index=5*/f32[384,384]{1,0:T(8,128)}) custom-call(s32[8,128]{1,0:T(8,128)} %bitcast.15, f32[8,128]{1,0:T(8,128)} %bitcast.16, bf16[128,1536]{1,0:T(8,128)(2,1)} %tok_ref.1, ...), custom_call_target="tpu_custom_call" | custom-call | flops 20000000000 | bytes 10000000 | tf_op jit(solution)/shard_map/pallas_call | solution.py:500
  187.8 2.6 %shard_map.119 = (bf16[128,1536]{1,0:T(8,128)(2,1)}, bf16[128,1536]{1,0:T(8,128)(2,1)}, f32[8,128]{1,0:T(8,128)}, f32[384,384]{1,0:T(8,128)}, f32[384,384]{1,0:T(8,128)}, /*index=5*/f32[384,384]{1,0:T(8,128)}) custom-call(bf16[128,1536]{1,0:T(8,128)(2,1)} %get-tuple-element.18.refs_0_, bf16[128,1536]{1,0:T(8,128)(2,1)} %get-tuple-element.19.refs_1_, ...), custom_call_target="tpu_custom_call" | custom-call | tf_op jit(solution)/shard_map/pallas_call | solution.py:556

commit v3 on v2

--- a/solution.py
+++ b/solution.py
@@ -52,11 +52,11 @@
 
 
 def kernel(
-    routes_ref, probs_ref, tok_ref, cot_ref, wg_hbm, wu_hbm, wd_hbm,
+    routes_ref, probs_ref, tok_hbm, cot_hbm, wg_hbm, wu_hbm, wd_hbm,
     out_ref, gtok_ref, gprob_ref, ogate_ref, oup_ref, odown_ref,
     wg, wu, wd, held, sent, rows_in, rows_back, xs, ss, hid, zback, wpart, perm, perm_t, psum,
     meta, meta_in, gs, gp_a, gp_b, gp_c, gp_d,
-    w_sem, z_send, z_recv, m_send, m_recv, y_send, y_recv, r_send, r_recv,
+    t_sem, w_sem, z_send, z_recv, m_send, m_recv, y_send, y_recv, r_send, r_recv,
     b_send, b_recv, x_send, x_recv, g_send, g_recv,
 ):
     mx = lax.axis_index("mirror")
@@ -82,16 +82,20 @@
     for k in range(1, 4):
         pl.semaphore_signal(barrier, inc=1, device_id=dev_x(k), device_id_type=MESH)
 
+    own = [
+        pltpu.make_async_copy(src.at[:, pl.ds(q * DQ, DQ)], held.at[0, a, pl.ds(q * T, T)], t_sem.at[a, q])
+        for a, src in enumerate((tok_hbm, cot_hbm))
+        for q in range(Q)
+    ]
+    for copy in own:
+        copy.start()
+
     weights = [
         pltpu.make_async_copy(src, dst, w_sem.at[n])
         for n, (src, dst) in enumerate(((wg_hbm, wg), (wu_hbm, wu), (wd_hbm, wd)))
     ]
     for copy in weights:
         copy.start()
-
-    for q in range(Q):
-        held[0, 0, q * T : (q + 1) * T, :] = tok_ref[:, q * DQ : (q + 1) * DQ]
-        held[0, 1, q * T : (q + 1) * T, :] = cot_ref[:, q * DQ : (q + 1) * DQ]
 
     row = iota((64, T), 0)
     expert = (((row & 7) >> 1) << 4) + ((row >> 3) << 1) + (row & 1)
@@ -109,22 +113,10 @@
         meta[p, 8:16, :] = weight[p * 8 : (p + 1) * 8, :]
     meta_in[0] = meta[z]
 
-    pl.semaphore_wait(barrier, 17)
-
     def remote(src, dst, send, recv, device):
         return pltpu.make_async_remote_copy(
             src_ref=src, dst_ref=dst, send_sem=send, recv_sem=recv, device_id=device, device_id_type=MESH
         )
-
-    for a in range(2):
-        for slot, step in ((1, 1), (2, -1)):
-            remote(held.at[0, a], held.at[slot, a], z_send.at[0], z_recv.at[slot, a], dev_z(step)).start()
-        if a == 0:
-            for i in range(1, 8):
-                to = -offsets[i]
-                remote(
-                    meta.at[(z + to + 8) % 8], meta_in.at[i], m_send.at[i], m_recv.at[i], dev_z(to)
-                ).start()
 
     r80 = iota((BLK, T), 0)
     q80 = div20(r80)
@@ -149,10 +141,7 @@
 
     def unit(i, a):
         s = i % 4
-
-        @pl.when(i >= 1)
-        def _():
-            wait(held.at[i, a], z_recv.at[i, a])
+        wait(held.at[i, a], z_recv.at[i, a])
 
         @pl.when((i >= 1) & (i <= 4))
         def _():
@@ -171,20 +160,26 @@
 
         if a == 0:
 
-            @pl.when(i >= 1)
-            def _():
-                wait(meta_in.at[i], m_recv.at[i])
-
+            wait(meta_in.at[i], m_recv.at[i])
+
+        @pl.when(i >= 4)
+        def _():
+            wait(sent.at[s, a, pl.ds(0, 7 * BLK)], y_send.at[s, a])
+
+        pick(i, a)
+        send_out(i, a)
+
+    def pick(i, a):
+        s = i % 4
         source = held[i, a]
         picked = sum(dot(m, source) for m in select(i, a == 1))
-
-        @pl.when(i >= 4)
-        def _():
-            wait(sent.at[s, a, pl.ds(0, 7 * BLK)], y_send.at[s, a])
-
         sent[s, a] = picked.astype(BF16)
         mine = pl.ds(pl.multiple_of(j * BLK, 16), BLK)
         rows_in[i, a, mine, :] = sent[s, a, mine, :]
+
+    def send_out(i, a):
+        s = i % 4
+        mine = pl.ds(pl.multiple_of(j * BLK, 16), BLK)
 
         def send(k, _):
             other = (j + k) % 8
@@ -246,15 +241,12 @@
 
         lax.fori_loop(1, 8, send, 0)
 
-    def give_group(g):
-        first, last = bounds(g)
-        for a in range(2):
-
-            def one(i, _, a=a):
-                give_back(i, a)
-                return 0
-
-            lax.fori_loop(first, last, one, 0)
+    def give(slots, a):
+        def one(n, _):
+            give_back(slots - n, a)
+            return 0
+
+        return one
 
     def bounds(g):
         return jnp.minimum(jnp.maximum(2 * g - 1, 0), 8), jnp.minimum(2 * g + 1, 8)
@@ -280,10 +272,6 @@
 
             lax.fori_loop(first, last, one, 0)
 
-        @pl.when(g == 0)
-        def _():
-            make_perms()
-
         @pl.when(g == 2)
         def _():
             for copy in weights:
@@ -306,7 +294,24 @@
 
         return 0
 
-    lax.fori_loop(0, 6, group, 0)
+    for a in range(2):
+        for copy in own[a * Q : (a + 1) * Q]:
+            copy.wait()
+        pick(0, a)
+    pl.semaphore_wait(barrier, 17)
+    send_out(0, 0)
+    for a in range(2):
+        for slot, step in ((1, 1), (2, -1)):
+            remote(held.at[0, a], held.at[slot, a], z_send.at[0], z_recv.at[slot, a], dev_z(step)).start()
+        if a == 0:
+            for i in range(1, 8):
+                to = -offsets[i]
+                remote(
+                    meta.at[(z + to + 8) % 8], meta_in.at[i], m_send.at[i], m_recv.at[i], dev_z(to)
+                ).start()
+    send_out(0, 1)
+    make_perms()
+    lax.fori_loop(1, 6, group, 0)
 
     row = iota((8 * ROWS, 128), 0)
     lanes = iota((8 * ROWS, 128), 1)
@@ -399,22 +404,32 @@
                 remote(held.at[half], zback.at[half], b_send.at[n], b_recv.at[n, a], dev_z(step)).start()
 
     def back(t, _):
-        g = 4 - t
-        first, last = bounds(g)
-
-        @pl.when((g >= 1) & (g <= 3))
-        def _():
-            give_group(g - 1)
+        first = jnp.where(t == 0, 7, jnp.where(t == 1, 6, jnp.where(t == 4, 0, 4)))
+        plain = jnp.where(t == 1, 2, 1)
+
+        @pl.when(t == 1)
+        def _():
+            lax.fori_loop(0, 4, give(4, 0), 0)
+
+        @pl.when(t == 2)
+        def _():
+            lax.fori_loop(0, 4, give(4, 1), 0)
+
+        @pl.when(t == 3)
+        def _():
+            for a in range(2):
+                give_back(0, a)
 
         for a in range(2):
-
-            def one(i, _, a=a):
-                back_unit(i, a)
+            count = jnp.where(t == 2 + a, 4, jnp.where(t == 3 - a, 0, plain))
+
+            def one(n, _, a=a):
+                back_unit(first - n, a)
                 return 0
 
-            lax.fori_loop(first, last, one, 0)
-
-        @pl.when(g == 3)
+            lax.fori_loop(0, count, one, 0)
+
+        @pl.when(t == 1)
         def _():
             wait(gp_b.at[pl.ds(0, 56)], g_recv.at[0])
             row = iota((64, 64), 0)
@@ -428,7 +443,7 @@
                     gp_c.at[pl.ds(i * 8, 8)], gp_d.at[own], g_send.at[1], g_recv.at[1], dev_z(offsets[i])
                 ).start()
 
-        @pl.when(g == 2)
+        @pl.when(t == 2)
         def _():
             wait(gp_d.at[pl.ds(0, 56)], g_recv.at[1])
             row = iota((64, T), 0)
@@ -443,7 +458,7 @@
                 found = jnp.sum(jnp.where(hit, dense, 0.0), axis=0, keepdims=True)
                 gprob_ref[k : k + 1, :] = found / probs_ref[k : k + 1, :]
 
-        @pl.when(g == 1)
+        @pl.when(t == 3)
         def _():
             for n in range(3):
                 wait(wpart.at[n], x_recv.at[n])
@@ -507,7 +522,7 @@
             jax.ShapeDtypeStruct((F, F), F32),
             jax.ShapeDtypeStruct((F, F), F32),
         ),
-        in_specs=[vmem] * 4 + [hbm] * 3,
+        in_specs=[vmem] * 2 + [hbm] * 5,
         out_specs=(vmem,) * 6,
         scratch_shapes=[
             pltpu.VMEM((D, F), BF16),
@@ -532,6 +547,7 @@
             pltpu.VMEM((64, 128), F32),
             pltpu.VMEM((64, 128), F32),
             pltpu.VMEM((64, 128), F32),
+            dma((2, Q)),
             dma((3,)),
             dma((7,)),
             dma((8, 2)),

time: 191 us -> 190 us (level)
  no operation moved by 1% of the time
where the time goes in v3:
time: 190 us
  Pallas kernels  189 us (99%)
    pallas_call x1, Pallas kernels, shards(): pl.pallas_call(kernel, out_shape=(jax.ShapeDtypeStruct((T, D), BF16), jax...  187 us

profile of v3, /device:TPU:1, one launch (start us, length us, event | category | flops | bytes accessed | tf_op | source)
XLA Modules:
  0.0 190.0 jit_solution(12642999056015401621)
XLA Ops:
  0.6 186.6 %shard_map.118 = (bf16[128,1536]{1,0:T(8,128)(2,1)}, bf16[128,1536]{1,0:T(8,128)(2,1)}, f32[8,128]{1,0:T(8,128)}, f32[384,384]{1,0:T(8,128)}, f32[384,384]{1,0:T(8,128)}, /*index=5*/f32[384,384]{1,0:T(8,128)}) custom-call(s32[8,128]{1,0:T(8,128)} %bitcast.15, f32[8,128]{1,0:T(8,128)} %bitcast.16, bf16[128,1536]{1,0:T(8,128)(2,1)} %tok_hbm.1, ...), custom_call_target="tpu_custom_call" | custom-call | flops 20000000000 | bytes 10000000 | tf_op jit(solution)/shard_map/pallas_call | solution.py:515
  187.3 2.6 %shard_map.119 = (bf16[128,1536]{1,0:T(8,128)(2,1)}, bf16[128,1536]{1,0:T(8,128)(2,1)}, f32[8,128]{1,0:T(8,128)}, f32[384,384]{1,0:T(8,128)}, f32[384,384]{1,0:T(8,128)}, /*index=5*/f32[384,384]{1,0:T(8,128)}) custom-call(bf16[128,1536]{1,0:T(8,128)(2,1)} %get-tuple-element.18.refs_0_, bf16[128,1536]{1,0:T(8,128)(2,1)} %get-tuple-element.19.refs_1_, ...), custom_call_target="tpu_custom_call" | custom-call | tf_op jit(solution)/shard_map/pallas_call | solution.py:572

commit v4 on v3

--- a/solution.py
+++ b/solution.py
@@ -56,7 +56,7 @@
     out_ref, gtok_ref, gprob_ref, ogate_ref, oup_ref, odown_ref,
     wg, wu, wd, held, sent, rows_in, rows_back, xs, ss, hid, zback, wpart, perm, perm_t, psum,
     meta, meta_in, gs, gp_a, gp_b, gp_c, gp_d,
-    t_sem, w_sem, z_send, z_recv, m_send, m_recv, y_send, y_recv, r_send, r_recv,
+    w_out, o_sem, t_sem, w_sem, z_send, z_recv, m_send, m_recv, y_send, y_recv, r_send, r_recv,
     b_send, b_recv, x_send, x_recv, g_send, g_recv,
 ):
     mx = lax.axis_index("mirror")
@@ -464,10 +464,12 @@
                 wait(wpart.at[n], x_recv.at[n])
             mine = sent[mx, :, 0:WROWS, :].astype(F32)
             total = ((mine + wpart[0].astype(F32)) + wpart[1].astype(F32)) + wpart[2].astype(F32)
-            ogate_ref[...] = jnp.transpose(total[0, 0:F])
-            oup_ref[...] = jnp.transpose(total[1, 0:F])
-            odown_ref[0 : F // 2, :] = total[0, F:WROWS]
-            odown_ref[F // 2 :, :] = total[1, F:WROWS]
+            w_out[0] = jnp.transpose(total[0, 0:F])
+            w_out[1] = jnp.transpose(total[1, 0:F])
+            w_out[2, 0 : F // 2, :] = total[0, F:WROWS]
+            w_out[2, F // 2 :, :] = total[1, F:WROWS]
+            for n, ref in enumerate((ogate_ref, oup_ref, odown_ref)):
+                pltpu.make_async_copy(w_out.at[n], ref, o_sem.at[n]).start()
 
         return 0
 
@@ -480,6 +482,8 @@
         for q in range(Q):
             ref[:, q * DQ : (q + 1) * DQ] = total[q * T : (q + 1) * T, :].astype(BF16)
 
+    for n in range(3):
+        wait(w_out.at[n], o_sem.at[n])
     wait(held.at[pl.ds(0, 2)], z_send.at[0])
     for i in range(1, 8):
         wait(meta.at[0], m_send.at[i])
@@ -523,7 +527,7 @@
             jax.ShapeDtypeStruct((F, F), F32),
         ),
         in_specs=[vmem] * 2 + [hbm] * 5,
-        out_specs=(vmem,) * 6,
+        out_specs=(vmem,) * 3 + (hbm,) * 3,
         scratch_shapes=[
             pltpu.VMEM((D, F), BF16),
             pltpu.VMEM((D, F), BF16),
@@ -547,6 +551,8 @@
             pltpu.VMEM((64, 128), F32),
             pltpu.VMEM((64, 128), F32),
             pltpu.VMEM((64, 128), F32),
+            pltpu.VMEM((3, F, F), F32),
+            dma((3,)),
             dma((2, Q)),
             dma((3,)),
             dma((7,)),

time: 190 us -> 189 us (level)
  no operation moved by 1% of the time
where the time goes in v4:
time: 189 us
  Pallas kernels  189 us (100%)
    pallas_call x1, Pallas kernels, shards(): pl.pallas_call(kernel, out_shape=(jax.ShapeDtypeStruct((T, D), BF16), jax...  186 us

profile of v4, /device:TPU:1, one launch (start us, length us, event | category | flops | bytes accessed | tf_op | source)
XLA Modules:
  0.0 189.3 jit_solution(17791005045784599787)
XLA Ops:
  0.6 186.1 %shard_map.118 = (bf16[128,1536]{1,0:T(8,128)(2,1)}, bf16[128,1536]{1,0:T(8,128)(2,1)}, f32[8,128]{1,0:T(8,128)}, f32[384,384]{1,0:T(8,128)}, f32[384,384]{1,0:T(8,128)}, /*index=5*/f32[384,384]{1,0:T(8,128)}) custom-call(s32[8,128]{1,0:T(8,128)} %bitcast.15, f32[8,128]{1,0:T(8,128)} %bitcast.16, bf16[128,1536]{1,0:T(8,128)(2,1)} %tok_hbm.1, ...), custom_call_target="tpu_custom_call" | custom-call | flops 20000000000 | bytes 10000000 | tf_op jit(solution)/shard_map/pallas_call | solution.py:519
  186.7 2.6 %shard_map.119 = (bf16[128,1536]{1,0:T(8,128)(2,1)}, bf16[128,1536]{1,0:T(8,128)(2,1)}, f32[8,128]{1,0:T(8,128)}, f32[384,384]{1,0:T(8,128)}, f32[384,384]{1,0:T(8,128)}, /*index=5*/f32[384,384]{1,0:T(8,128)}) custom-call(bf16[128,1536]{1,0:T(8,128)(2,1)} %get-tuple-element.18.refs_0_, bf16[128,1536]{1,0:T(8,128)(2,1)} %get-tuple-element.19.refs_1_, ...), custom_call_target="tpu_custom_call" | custom-call | tf_op jit(solution)/shard_map/pallas_call | solution.py:578
